TPU v7x, 32 devices: a whole 2x2x4 slice. The times are simulated.
32 devices in a mesh: freq: 2 (over y), src: 4 (over z), tgt: 2 (over x), pol: 2 (over core).
Axes of the slice: x: 2, y: 2, z: 4, core: 2. Of those that a mesh axis runs over, the one named last changes fastest.
Arguments:
- sub_points: float32 [3, 4096], P(None, 'src'), may hold values from -1 to 1
- sub_currents: bfloat16 [2, 4096, 128], P('pol', 'src'), may hold values from -6 to 6
- main_points: float32 [3, 1024], P(None, ('src', 'tgt')), may hold values from 2 to 6
- main_weight: float32 [1024], P(('src', 'tgt')), may hold values from 0.3 to 3
- panel_ids: int32 [1024], P(('src', 'tgt')), may hold values from 0 to 63
- panel_shift: float32 [64], replicated, may hold values from -0.05 to 0.05
- theta: float32 [128], replicated, may hold values from 0 to 0.6
- phi: float32 [128], replicated, may hold values from -3.140625 to 3.140625
- wavenumber: float32 [2], P('freq'), parts along dimension 0, may hold values from 20 to 60
Outputs:
- main_current: bfloat16 [2, 1024, 256], P('pol', ('src', 'tgt'), 'freq'), parts along dimension 2
- far_field: float32 [2, 128, 256], P('pol', ('src', 'tgt'), 'freq'), parts along dimension 2
There are 2 independent parts, one for each index of `freq`. A program takes and returns all parts, laid end to end along the dimension named above; an argument that names none is the same for every part. Nothing has to cross between parts.
All inputs are finite; a program needn't handle non-finite values.
Results may differ from a plain program's by a relative error of at most 0.0056.
Values may be sent and summed in bfloat16 or wider, within the bound.
A program may use at most 64 MiB of HBM per device.

v0:
```python
import math

import jax
import jax.numpy as jnp
from jax import lax
from jax.sharding import PartitionSpec as P


def from_partner(value, axis, apart):
    mask = 2**apart
    pairs = [(source, source ^ mask) for source in range(lax.axis_size(axis))]
    return lax.ppermute(value, axis, pairs)


def blockwise(worker, points):
    total_rows = points.shape[1]
    block_rows = 512
    if total_rows > block_rows and total_rows % block_rows == 0:
        blocks = points.reshape(3, total_rows // block_rows, block_rows).transpose(1, 0, 2)
        result = lax.map(worker, blocks)
        return result.reshape(total_rows, result.shape[-1])
    return worker(points)


def rotated(current):
    half_cols = current.shape[1] // 2
    lower = jnp.concatenate([-current[:, half_cols:], current[:, :half_cols]], 1)
    return jnp.concatenate([current, lower], 0)


def near_kernel(targets, sources, wave_number):
    differ = targets[0][:, None] - sources[0][None, :]
    square = differ * differ
    differ = targets[1][:, None] - sources[1][None, :]
    square = square + differ * differ
    differ = targets[2][:, None] - sources[2][None, :]
    square = square + differ * differ
    radius = jnp.sqrt(square)
    phase = wave_number * radius
    real_part = (4.0 * jnp.cos(phase) / radius).astype(jnp.bfloat16)
    imag_part = (-4.0 * jnp.sin(phase) / radius).astype(jnp.bfloat16)
    return jnp.concatenate([real_part, imag_part], 1)


def far_kernel(unit_dirs, sources, wave_number):
    inner = (
        unit_dirs[0][:, None] * sources[0][None, :] + unit_dirs[1][:, None] * sources[1][None, :]
    )
    inner = inner + unit_dirs[2][:, None] * sources[2][None, :]
    phase = wave_number * inner
    real_part = jnp.cos(phase).astype(jnp.bfloat16)
    imag_part = jnp.sin(phase).astype(jnp.bfloat16)
    return jnp.concatenate([real_part, imag_part], 1)


def currents_from(induced, weight, angle):
    half_cols = induced.shape[1] // 2
    real_in = induced[:, :half_cols]
    imag_in = induced[:, half_cols:]
    cosine = jnp.cos(angle)[:, None]
    sine = jnp.sin(angle)[:, None]
    real_out = weight[:, None] * (real_in * cosine + imag_in * sine)
    imag_out = weight[:, None] * (imag_in * cosine - real_in * sine)
    return jnp.concatenate([real_out, imag_out], 1).astype(jnp.bfloat16)


def on_device(
    sub_points,
    sub_currents,
    main_points,
    main_weight,
    panel_ids,
    panel_shift,
    theta,
    phi,
    wavenumber,
):
    wave_number = wavenumber[0]
    src_count = lax.axis_size("src")
    tgt_count = lax.axis_size("tgt")
    main_rows = main_points.shape[1]
    dir_rows = theta.shape[0] // (src_count * tgt_count)
    sub_total = sub_points.shape[1] * src_count
    main_total = main_rows * src_count * tgt_count
    near_weights = rotated(sub_currents[0])
    block_points = lax.all_gather(main_points, "src", axis=1, tiled=True)

    def first_section(points_block):
        return jnp.dot(
            near_kernel(points_block, sub_points, wave_number),
            near_weights,
            preferred_element_type=jnp.float32,
        )

    induced = lax.psum_scatter(
        blockwise(first_section, block_points), "src", scatter_dimension=0, tiled=True
    ) * (1.0 / math.sqrt(sub_total))
    panel_range = jnp.arange(panel_shift.shape[0], dtype=jnp.int32)
    chosen = jnp.sum(
        jnp.where(panel_ids[:, None] == panel_range[None, :], panel_shift[None, :], 0.0), 1
    )
    current = currents_from(induced, main_weight, 2.0 * wave_number * chosen)
    unit_dirs = jnp.stack(
        [jnp.sin(theta) * jnp.cos(phi), jnp.sin(theta) * jnp.sin(phi), jnp.cos(theta)], 0
    )
    wide_current = lax.all_gather(current, "tgt", axis=0, tiled=True)
    group_points = lax.all_gather(main_points, "tgt", axis=1, tiled=True)
    far_weights = rotated(wide_current)
    arranged = unit_dirs.reshape(3, src_count, tgt_count, dir_rows)
    tgt_dirs = lax.dynamic_index_in_dim(arranged, lax.axis_index("tgt"), 2, keepdims=False).reshape(
        3, src_count * dir_rows
    )

    def second_section(points_block):
        return jnp.dot(
            far_kernel(points_block, group_points, wave_number),
            far_weights,
            preferred_element_type=jnp.float32,
        )

    radiated = lax.psum_scatter(
        blockwise(second_section, tgt_dirs), "src", scatter_dimension=0, tiled=True
    )
    radiated = radiated * (1.0 / math.sqrt(main_total))
    partner = from_partner(radiated, "pol", 0)
    own_start = (lax.axis_index("src") * tgt_count + lax.axis_index("tgt")) * dir_rows
    own_phi = lax.dynamic_slice_in_dim(phi, own_start, dir_rows, 0)
    cos_phi = jnp.cos(own_phi)[:, None]
    sin_phi = jnp.sin(own_phi)[:, None]
    sign_flip = 1.0 - 2.0 * lax.axis_index("pol").astype(jnp.float32)
    combined = cos_phi * radiated + sign_flip * sin_phi * partner
    return (current[None], combined[None])


def solution(mesh):
    placed = (
        P(None, "src"),
        P("pol", "src", None),
        P(None, ("src", "tgt")),
        P(("src", "tgt")),
        P(("src", "tgt")),
        P(),
        P(),
        P(),
        P("freq"),
    )
    return jax.shard_map(
        on_device,
        mesh=mesh,
        in_specs=placed,
        out_specs=(P("pol", ("src", "tgt"), "freq"), P("pol", ("src", "tgt"), "freq")),
        check_vma=False,
    )
```

profile of v0, /device:TPU:0, one launch (start us, length us, event | category | flops | bytes accessed | tf_op | source)
XLA Modules:
  0.0 88.2 jit_solution(12491903438195029217)
XLA Ops:
  7.2 0.0 reduce-scatter.3.cloned.1.call-start
  7.2 13.7 %all_gather.9 = f32[3,512]{1,0:T(4,128)S(1)} all-gather(f32[3,128]{1,0:T(4,128)} %param.11), channel_id=1, replica_groups=mesh['freq'=2,'src'=4,'tgt'=2,'pol'=2] {'src'}, dimensions={1}, use_global_device_ids=true | all-gather | bytes 7680 | tf_op jit(solution)/shard_map/all_gather | solution.py:86
  20.9 0.8 fusion.22
  22.4 1.2 %slice_negate_fusion = (bf16[1024,64]{1,0:T(8,128)(2,1)S(1)}, bf16[1024,64]{1,0:T(8,128)(2,1)S(1)}) fusion(bf16[1024,128]{1,0:T(8,128)(2,1)} %bitcast.18), kind=kLoop, calls=%fused_computation.12 | loop fusion | flops 65536 | bytes 524288 | tf_op jit(solution)/shard_map/neg | solution.py:27
  23.6 9.4 %divide_convert_fusion.1 = (bf16[512,1024]{1,0:T(8,128)(2,1)S(1)}, bf16[512,1024]{1,0:T(8,128)(2,1)S(1)}) fusion(f32[1024]{0:T(1024)S(1)} %bitcast.26, f32[512]{0:T(512)S(1)} %bitcast.29, f32[1024]{0:T(1024)S(1)} %bitcast.27, f32[512]{0:T(512)S(1)} %bitcast.30, f32[1024]{0:T(1024)S(1)} %bitcast.25, f32[512]{0:T(512)S(1)} %bitcast.28, f32[]{:T(128)} %bitcast.15), kind=kLoop, calls=%fused_computation.5 | loop fusion | flops 7864320 | bytes 2115588 | tf_op jit(solution)/shard_map/convert_element_type | solution.py:40
  33.1 1.5 %fusion = f32[512,128]{1,0:T(8,128)} fusion(bf16[512,1024]{1,0:T(8,128)(2,1)S(1)} %get-tuple-element.12, bf16[512,1024]{1,0:T(8,128)(2,1)S(1)} %get-tuple-element.11, bf16[1024,64]{1,0:T(8,128)(2,1)S(1)} %get-tuple-element.6, bf16[1024,64]{1,0:T(8,128)(2,1)S(1)} %get-tuple-element.5, bf16[1024,128]{1,0:T(8,128)(2,1)S(1)} %bitcast.19), kind=kOutput, calls=%fused_computation | convolution fusion | flops 274202624 | bytes 2883584 | tf_op jit(solution)/shard_map/dot_general | solution.py:89
  34.6 0.0 reduce-scatter.3.cloned.1.call-update
  34.6 0.0 reduce-scatter.5.cloned.1.call-start
  34.8 0.1 stack.12
  34.9 0.1 stack.13
  34.9 0.1 stack.14
  35.0 0.0 copy-done.6
  35.1 0.1 select_reduce_fusion
  35.3 0.1 mul.222
  35.3 0.1 mul.227
  35.4 0.1 mul.232
  35.5 4.3 %all_gather.10 = f32[3,256]{1,0:T(4,128)S(1)} all-gather(f32[3,128]{1,0:T(4,128)S(1)} %copy-done.1), channel_id=1, replica_groups=mesh['freq'=2,'src'=4,'tgt'=2,'pol'=2] {'tgt'}, dimensions={1}, use_global_device_ids=true | all-gather | bytes 4608 | tf_op jit(solution)/shard_map/all_gather | solution.py:107
  39.8 0.3 cosine_convert_fusion
  40.2 14.0 %reduce-scatter.3.cloned.1.call-done = f32[128,128]{1,0:T(8,128)} async-done(((f32[512,128]{1,0:T(8,128)}), f32[128,128]{1,0:T(8,128)}) %reduce-scatter.3.cloned.1.call-update) | async-done | bytes 65552 | tf_op jit(solution)/shard_map/reduce_scatter | solution.py:95
  54.1 0.8 broadcast_multiply_fusion
  55.0 0.1 multiply_convert_fusion.1
  55.1 0.1 pad_maximum_fusion.1
  55.2 4.6 %all_gather.11 = bf16[256,128]{1,0:T(8,128)(2,1)S(1)} all-gather(bf16[128,128]{1,0:T(8,128)(2,1)S(1)} %pad_maximum_fusion.1), channel_id=1, replica_groups=mesh['freq'=2,'src'=4,'tgt'=2,'pol'=2] {'tgt'}, dimensions={0}, use_global_device_ids=true | all-gather | bytes 98304 | tf_op jit(solution)/shard_map/all_gather | solution.py:106
  59.8 0.1 slice_negate_fusion.1
  59.9 0.8 fusion.9
  60.7 0.0 reduce-scatter.5.cloned.1.call-update
  60.8 0.1 cosine_multiply_fusion
  60.9 17.2 %reduce-scatter.5.cloned.1.call-done = f32[16,128]{1,0:T(8,128)} async-done(((f32[64,128]{1,0:T(8,128)}), f32[16,128]{1,0:T(8,128)}) %reduce-scatter.5.cloned.1.call-update) | async-done | bytes 8208 | tf_op jit(solution)/shard_map/reduce_scatter | solution.py:121
  78.1 0.7 broadcast_multiply_fusion.1
  78.8 0.7 pad_maximum_fusion
  79.5 0.5 collective-permute-done
  80.0 1.4 %add_bitcast_fusion = f32[1,16,128]{2,1,0:T(8,128)} fusion(f32[16,128]{1,0:T(8,128)S(1)} %collective-permute-done, f32[16,128]{1,0:T(8,128)} %reduce-scatter.5.cloned.1.call-done, f32[16]{0:T(128)S(1)} %get-tuple-element.27, f32[16]{0:T(128)S(1)} %get-tuple-element.26), kind=kLoop, calls=%fused_computation.36 | loop fusion | flops 6144 | bytes 24704 | tf_op jit(solution)/shard_map/broadcast_in_dim | solution.py:132
  (21 shorter events, 0.2 us)
Async XLA Ops:
  7.2 47.0 %reduce-scatter.3.cloned.1.call-start = ((), (), s32[]{:S(2)}) async-start(), calls=%async_computation.2 | async-start | bytes 327680 | tf_op jit(solution)/shard_map/reduce_scatter | solution.py:95
  23.6 9.5 %copy-start = (bf16[1,1024,128]{2,1,0:T(8,128)(2,1)S(1)}, bf16[1,1024,128]{2,1,0:T(8,128)(2,1)}, u32[]{:S(2)}) copy-start(bf16[1,1024,128]{2,1,0:T(8,128)(2,1)} %param.10) | copy-start | bytes 786436
  33.1 1.6 %copy-start.4 = (f32[128]{0:T(128)S(1)}, f32[128]{0:T(128)}, u32[]{:S(2)}) copy-start(f32[128]{0:T(128)} %param.15) | copy-start | bytes 1540
  33.1 1.7 %copy-start.2 = (f32[128]{0:T(128)S(1)}, f32[128]{0:T(128)}, u32[]{:S(2)}) copy-start(f32[128]{0:T(128)} %param.16) | copy-start | bytes 1540
  33.1 2.0 %copy-start.5 = (f32[64]{0:T(128)S(1)}, f32[64]{0:T(128)}, u32[]{:S(2)}) copy-start(f32[64]{0:T(128)} %param.14) | copy-start | bytes 772
  33.1 2.0 %copy-start.6 = (s32[128]{0:T(128)S(1)}, s32[128]{0:T(128)}, u32[]{:S(2)}) copy-start(s32[128]{0:T(128)} %param.13) | copy-start | bytes 1540
  33.1 2.4 %copy-start.1 = (f32[3,128]{1,0:T(4,128)S(1)}, f32[3,128]{1,0:T(4,128)}, u32[]{:S(2)}) copy-start(f32[3,128]{1,0:T(4,128)} %param.11) | copy-start | bytes 4612
  33.1 21.9 %copy-start.3 = (f32[128]{0:T(128)S(1)}, f32[128]{0:T(128)}, u32[]{:S(2)}) copy-start(f32[128]{0:T(128)} %param.12) | copy-start | bytes 1540
  34.6 43.5 %reduce-scatter.5.cloned.1.call-start = ((), (), s32[]{:S(2)}) async-start(), calls=%async_computation.3 | async-start | bytes 40960 | tf_op jit(solution)/shard_map/reduce_scatter | solution.py:121
  78.8 1.2 %collective-permute-start = (f32[16,128]{1,0:T(8,128)S(1)}, f32[16,128]{1,0:T(8,128)S(1)}, u32[]{:S(2)}, u32[]{:S(2)}) collective-permute-start(f32[16,128]{1,0:T(8,128)S(1)} %broadcast_multiply_fusion.1), channel_id=1, source_target_pairs={{0,1},{1,0},{2,3},{3,2},{4,5},{5,4},{6,7},{7,6},{8,9},{9,8},{10,11... | collective-permute-start | bytes 24584 | tf_op jit(solution)/shard_map/ppermute | solution.py:12
Sparse Core Ops, SparseCore 0:
  34.7 19.3 reduce-scatter.2
  60.9 17.2 reduce-scatter.4
where the time goes:
time: 88.6 us; the launch traced here: 88.2 us
  waiting for transfers between devices  31.7 us (36%)
  blocking collectives  22.6 us (26%)
  other arithmetic  15.2 us (17%)
  between operations  14.8 us (17%)
  matrix products  2.31 us (3%)
  local copies, waits for them, and re-layouts  1.48 us (2%)
    reduce_scatter x1, waiting for transfers between devices, on_device(): lax.psum_scatter(blockwise(second_section, tgt_dirs), 'src', scatter_dime...  17.2 us
    reduce_scatter x1, waiting for transfers between devices, on_device(): lax.psum_scatter(blockwise(first_section, block_points), 'src', scatter_d...  14 us
    all_gather x1, blocking collectives, on_device(): block_points = lax.all_gather(main_points, 'src', axis=1, tiled=True)  13.7 us
    convert_element_type x1, other arithmetic, near_kernel(): real_part = (4.0 * jnp.cos(phase) / radius).astype(jnp.bfloat16)  9.44 us
    all_gather x1, blocking collectives, on_device(): wide_current = lax.all_gather(current, 'tgt', axis=0, tiled=True)  4.59 us
    all_gather x1, blocking collectives, on_device(): group_points = lax.all_gather(main_points, 'tgt', axis=1, tiled=True)  4.33 us
  transfers between devices with their start and end apart: 3, of which 3 were waited for; matrix products, arithmetic and copies ran while one was open for 2% of the time, Pallas kernels for 0%

commit v1 on v0

v1 whole, which is shorter than its diff:
```python
import functools
import math

import jax
import jax.numpy as jnp
from jax import lax
from jax.experimental import pallas as pl
from jax.experimental.pallas import tpu as pltpu
from jax.sharding import PartitionSpec as P

MESH = pl.DeviceIdType.MESH
TURN = 2.0 * math.pi
COS_HALF = (1.4142135381698608, -6.978850841522217, 5.739460468292236, -1.8835580348968506, 0.3106880187988281)
SIN_HALF = (4.442879676818848, -7.307816505432129, 3.5977745056152344, -0.7911993861198425)


def poly(coefs, s):
    value = coefs[-1]
    for coef in coefs[-2::-1]:
        value = value * s + coef
    return value


def turn_cos_sin(t):
    f = t - jnp.round(t)
    s = f * f
    half_cos = poly(COS_HALF, s)
    half_sin = f * poly(SIN_HALF, s)
    return 1.0 - half_sin * half_sin, half_cos * half_sin


def each(count, body, start=0):
    if count <= 16:
        for i in range(start, count):
            body(i)
    else:
        lax.fori_loop(start, count, lambda i, c: (body(i), c)[1], 0)


def thirds(x):
    first = x.astype(jnp.bfloat16).astype(jnp.float32)
    rest = x - first
    second = rest.astype(jnp.bfloat16).astype(jnp.float32)
    return first, second, rest - second


def left_rows(x):
    a, b, c = thirds(x)
    return jnp.concatenate([a, a, b, b, a, c], 0)


def right_rows(x):
    a, b, c = thirds(x)
    return jnp.concatenate([a, b, a, b, c, a], 0).astype(jnp.bfloat16)


def stack_rows(rows):
    n = rows[0].shape[1]
    index = lax.broadcasted_iota(jnp.int32, (8, n), 0)
    out = jnp.zeros((8, n), jnp.float32)
    for i, row in enumerate(rows):
        out = jnp.where(index == i, row, out)
    return out


def columns(rows):
    return jnp.transpose(stack_rows(rows))


def inner(left, right):
    lhs = jnp.transpose(left_rows(left)).astype(jnp.bfloat16)
    return jnp.dot(lhs, right_rows(right), preferred_element_type=jnp.float32)


def swapped(x):
    return pltpu.roll(x, x.shape[1] // 2, 1)


def kernel(
    S, T, sub_total, main_total,
    wave, sub_pts, sub_cur, main_pts, weight, ids, shift, theta, phi,
    cur_out, far_out,
    v_sub, v_cur, v_pts, v_weight, v_ids, v_shift, v_theta, v_phi,
    r2, kern, fkern, part, part_in, rad_own, rad_out, rad_in, phi_cols, cur_cols,
    in_sem, a_send, a_recv, b_send, b_recv, c_send, c_recv,
):
    rows = main_pts.shape[1]
    subs = sub_pts.shape[1]
    dirs = theta.shape[1]
    cols = sub_cur.shape[2]
    src, tgt, pol = lax.axis_index("src"), lax.axis_index("tgt"), lax.axis_index("pol")
    N = S * T * 2
    own_rows = dirs // (S * T)
    flat = (src * T + tgt) * 2 + pol

    def member(d):
        other = lax.rem(flat + d, N)
        return other, {"src": other // (T * 2), "tgt": lax.rem(other // 2, T), "pol": lax.rem(other, 2)}

    barrier = pltpu.get_barrier_semaphore()

    def greet(d):
        pl.semaphore_signal(barrier, inc=1, device_id=member(d)[1], device_id_type=MESH)

    each(N, greet, 1)

    loads = [
        pltpu.make_async_copy(a, b, in_sem.at[i])
        for i, (a, b) in enumerate([
            (main_pts, v_pts.at[0]), (sub_pts, v_sub), (theta, v_theta), (phi, v_phi),
            (weight, v_weight), (ids, v_ids), (shift, v_shift), (sub_cur.at[0], v_cur),
        ])
    ]
    for load in loads:
        load.start()
    pl.semaphore_wait(barrier, N - 1)

    def to_owner(d):
        return {"src": lax.rem(src + S - d, S)}

    def send_points(d):
        pltpu.make_async_remote_copy(
            main_pts, v_pts.at[d], a_send.at[d], a_recv.at[d],
            device_id={"src": lax.rem(src + d, S)}, device_id_type=MESH,
        ).start()

    each(S, send_points, 1)

    q = wave[0] * (1.0 / TURN)
    low_half = lax.broadcasted_iota(jnp.int32, (1, cols), 1) < cols // 2
    sign = jnp.where(low_half, 1.0, -1.0)

    for load in loads[:2]:
        load.wait()
    sx, sy, sz = (v_sub[i : i + 1, :] * q for i in range(3))
    one = jnp.ones_like(sx)
    sub_side = right_rows(stack_rows([sx, sy, sz, one, sx * sx + sy * sy + sz * sz]))

    def near_block(d, slot):
        x, y, z = (v_pts[d, i : i + 1, :] * q for i in range(3))
        main_side = stack_rows(
            [-2.0 * x, -2.0 * y, -2.0 * z, x * x + y * y + z * z, jnp.ones_like(x)]
        )
        r2[slot] = inner_with(main_side, sub_side)
        step = 16
        for at in range(0, rows, step):
            square = r2[slot, at : at + step, :]
            inverse = lax.rsqrt(square)
            cosine, sine = turn_cos_sin(square * inverse)
            kern[slot, at : at + step, :] = (cosine * inverse).astype(jnp.bfloat16)
            kern[slot, rows + at : rows + at + step, :] = (sine * inverse).astype(jnp.bfloat16)
        both = jnp.dot(kern[slot], v_cur[...], preferred_element_type=jnp.float32)
        return both[:rows] + sign * swapped(both[rows:])

    def inner_with(left, right):
        lhs = jnp.transpose(left_rows(left)).astype(jnp.bfloat16)
        return jnp.dot(lhs, right, preferred_element_type=jnp.float32)

    for load in loads[2:]:
        load.wait()
    cos_t, sin_t = turn_cos_sin(v_theta[...] * (1.0 / TURN))
    cos_p, sin_p = turn_cos_sin(v_phi[...] * (1.0 / TURN))
    phi_cols[...] = columns([cos_p, sin_p])
    units = stack_rows([sin_t * cos_p, sin_t * sin_p, cos_t])
    px, py, pz = (v_pts[0, i : i + 1, :] * q for i in range(3))
    unit_side = jnp.transpose(left_rows(units)).astype(jnp.bfloat16)
    turns = jnp.dot(
        unit_side, right_rows(stack_rows([px, py, pz])), preferred_element_type=jnp.float32
    )
    step = 128
    for at in range(0, dirs, step):
        cosine, sine = turn_cos_sin(turns[at : at + step])
        fkern[at : at + step, :] = cosine.astype(jnp.bfloat16)
        fkern[dirs + at : dirs + at + step, :] = sine.astype(jnp.bfloat16)

    cols_in = columns([v_weight[...], v_ids[...].astype(jnp.float32)])
    panel = lax.broadcasted_iota(jnp.int32, (rows, shift.shape[1]), 1).astype(jnp.float32)
    chosen = jnp.sum(jnp.where(cols_in[:, 1:2] == panel, v_shift[...], 0.0), 1, keepdims=True)
    cos_a, sin_a = turn_cos_sin(jnp.broadcast_to(2.0 * q * chosen, (rows, cols)))
    scale = 4.0 * q * (1.0 / math.sqrt(sub_total))
    factor = scale * cols_in[:, 0:1]
    cur_cols[0] = factor * cos_a
    cur_cols[1] = factor * sin_a * sign

    own = near_block(0, 0)

    def remote_block(d):
        pltpu.make_async_remote_copy(
            main_pts, v_pts.at[d], a_send.at[d], a_recv.at[d],
            device_id=to_owner(d), device_id_type=MESH,
        ).wait()
        part[d] = near_block(d, d % 2).astype(jnp.bfloat16)
        pltpu.make_async_remote_copy(
            part.at[d], part_in.at[d], b_send.at[d], b_recv.at[d],
            device_id=to_owner(d), device_id_type=MESH,
        ).start()

    each(S, remote_block, 1)

    def landed(d):
        pltpu.make_async_remote_copy(
            part.at[d], part_in.at[d], b_send.at[d], b_recv.at[d],
            device_id=to_owner(d), device_id_type=MESH,
        ).wait()

    each(S, landed, 1)
    induced = own
    if S <= 16:
        for d in range(1, S):
            induced = induced + part_in[d].astype(jnp.float32)
    else:
        induced = lax.fori_loop(
            1, S, lambda d, total: total + part_in[d].astype(jnp.float32), induced
        )
    current = (induced * cur_cols[0] + swapped(induced) * cur_cols[1]).astype(jnp.bfloat16)
    cur_out[0] = current

    for at in range(0, dirs, step):
        real = jnp.dot(fkern[at : at + step], current, preferred_element_type=jnp.float32)
        imag = jnp.dot(
            fkern[dirs + at : dirs + at + step], current, preferred_element_type=jnp.float32
        )
        field = real - sign * swapped(imag)
        rad_own[at : at + step] = field
        rad_out[at : at + step] = field.astype(jnp.bfloat16)

    def far_copy(d):
        other, where = member(d)
        first = pl.multiple_of(other // 2 * own_rows, own_rows)
        return pltpu.make_async_remote_copy(
            rad_out.at[pl.ds(first, own_rows)], rad_in.at[d], c_send.at[d], c_recv.at[d],
            device_id=where, device_id_type=MESH,
        )

    each(N, lambda d: far_copy(d).start(), 1)
    each(N, lambda d: far_copy(d).wait(), 1)

    here = pl.ds(pl.multiple_of((src * T + tgt) * own_rows, own_rows), own_rows)
    mine = rad_own[here]
    theirs = rad_in[1].astype(jnp.float32)

    def gathered(d, pair):
        return (
            pair[0] + rad_in[2 * d].astype(jnp.float32),
            pair[1] + rad_in[2 * d + 1].astype(jnp.float32),
        )

    if N <= 16:
        for d in range(1, N // 2):
            mine, theirs = gathered(d, (mine, theirs))
    else:
        mine, theirs = lax.fori_loop(1, N // 2, gathered, (mine, theirs))
    angles = phi_cols[here]
    flip = 1.0 - 2.0 * pol.astype(jnp.float32)
    far_out[0] = (angles[:, 0:1] * mine + (flip * angles[:, 1:2]) * theirs) * (
        1.0 / math.sqrt(main_total)
    )


def on_device(S, T, sub_points, sub_currents, main_points, main_weight, panel_ids, panel_shift, theta, phi, wavenumber):
    rows, subs = main_points.shape[1], sub_points.shape[1]
    cols = sub_currents.shape[2]
    dirs = theta.shape[0]
    panels = panel_shift.shape[0]
    N = S * T * 2
    own_rows = dirs // (S * T)
    f32, bf16 = jnp.float32, jnp.bfloat16
    hbm = pl.BlockSpec(memory_space=pl.ANY)
    vmem = pl.BlockSpec(memory_space=pltpu.VMEM)
    dma = pltpu.SemaphoreType.DMA
    return pl.pallas_call(
        functools.partial(kernel, S, T, subs * S, rows * S * T),
        out_shape=(
            jax.ShapeDtypeStruct((1, rows, cols), bf16),
            jax.ShapeDtypeStruct((1, own_rows, cols), f32),
        ),
        in_specs=[pl.BlockSpec(memory_space=pltpu.SMEM)] + [hbm] * 8,
        out_specs=(vmem, vmem),
        scratch_shapes=[
            pltpu.VMEM((3, subs), f32),
            pltpu.VMEM((subs, cols), bf16),
            pltpu.VMEM((S, 3, rows), f32),
            pltpu.VMEM((1, rows), f32),
            pltpu.VMEM((1, rows), jnp.int32),
            pltpu.VMEM((1, panels), f32),
            pltpu.VMEM((1, dirs), f32),
            pltpu.VMEM((1, dirs), f32),
            pltpu.VMEM((2, rows, subs), f32),
            pltpu.VMEM((2, 2 * rows, subs), bf16),
            pltpu.VMEM((2 * dirs, rows), bf16),
            pltpu.VMEM((S, rows, cols), bf16),
            pltpu.VMEM((S, rows, cols), bf16),
            pltpu.VMEM((dirs, cols), f32),
            pltpu.VMEM((dirs, cols), bf16),
            pltpu.VMEM((N, own_rows, cols), bf16),
            pltpu.VMEM((dirs, 8), f32),
            pltpu.VMEM((2, rows, cols), f32),
            dma((8,)),
            dma((S,)),
            dma((S,)),
            dma((S,)),
            dma((S,)),
            dma((N,)),
            dma((N,)),
        ],
        compiler_params=pltpu.CompilerParams(
            collective_id=0, has_side_effects=True, vmem_limit_bytes=32 * 1024 * 1024
        ),
    )(
        wavenumber, sub_points, sub_currents, main_points, main_weight.reshape(1, -1),
        panel_ids.reshape(1, -1), panel_shift.reshape(1, -1), theta.reshape(1, -1), phi.reshape(1, -1),
    )


def solution(mesh):
    placed = (
        P(None, "src"),
        P("pol", "src", None),
        P(None, ("src", "tgt")),
        P(("src", "tgt")),
        P(("src", "tgt")),
        P(),
        P(),
        P(),
        P("freq"),
    )
    return jax.shard_map(
        functools.partial(on_device, mesh.shape["src"], mesh.shape["tgt"]),
        mesh=mesh,
        in_specs=placed,
        out_specs=(P("pol", ("src", "tgt"), "freq"), P("pol", ("src", "tgt"), "freq")),
        check_vma=False,
    )
```

time: 88.6 us -> 23.8 us (0.27)
  waiting for transfers between devices: 31.7 us -> 0 us
  blocking collectives: 22.6 us -> 0 us
  Pallas kernels: 0 us -> 18.7 us
  other arithmetic: 15.2 us -> 0 us
  between operations: 14.8 us -> 1.34 us
  matrix products: 2.31 us -> 0 us
  local copies, waits for them, and re-layouts: 1.48 us -> 3.57 us
    reduce_scatter x2 -> x0, waiting for transfers between devices: 31.2 us -> none  [the longest x1 17.2 us: on_device(): lax.psum_scatter(blockwise(second_section, tgt_dirs), 'src', scatter_dime...]
    all_gather x3 -> x0, blocking collectives: 22.6 us -> none  [the longest x1 13.7 us: on_device(): block_points = lax.all_gather(main_points, 'src', axis=1, tiled=True)]
    pallas_call x0 -> x1, Pallas kernels: none -> 18.7 us  [on_device(): pl.pallas_call(functools.partial(kernel, S, T, subs * S, rows * S * T), o...]
    convert_element_type x2 -> x0, other arithmetic: 9.77 us -> none  [the longest x1 9.44 us: near_kernel(): real_part = (4.0 * jnp.cos(phase) / radius).astype(jnp.bfloat16)]
    unnamed x14 -> x18, local copies, waits for them, and re-layouts: 0.05 us -> 3.57 us
    dot_general x2 -> x0, matrix products: 2.31 us -> none  [the longest x1 1.46 us: first_section(): jnp.dot(near_kernel(points_block, sub_points, wave_number), near_weights,...]
    mul x4 -> x0, other arithmetic: 1.7 us -> none  [the longest x1 0.84 us: on_device(): lax.psum_scatter(blockwise(first_section, block_points), 'src', scatter_d...]
    broadcast_in_dim x1 -> x0, other arithmetic: 1.37 us -> none  [on_device(): return (current[None], combined[None])]
  transfers between devices with their start and end apart: 3 -> 0, of which waited for: 3 -> 0; matrix products, arithmetic and copies ran while one was open for 2% -> 0% of each run, Pallas kernels for 0% -> 0%
where the time goes in v1:
time: 23.8 us; the launch traced here: 23.6 us
  Pallas kernels  18.7 us (79%)
  local copies, waits for them, and re-layouts  3.57 us (15%)
  between operations  1.34 us (6%)
    pallas_call x1, Pallas kernels, on_device(): pl.pallas_call(functools.partial(kernel, S, T, subs * S, rows * S * T), o...  18.7 us
    unnamed x18, local copies, waits for them, and re-layouts  3.57 us

profile of v1, /device:TPU:0, one launch (start us, length us, event | category | flops | bytes accessed | tf_op | source)
XLA Modules:
  0.0 23.6 jit_solution(16813671957244264424)
XLA Ops:
  1.3 0.0 copy-start.6
  1.3 0.0 copy-start.7
  1.3 0.0 copy-start.2
  1.3 0.0 copy-start.3
  1.3 0.0 copy-start.4
  1.3 0.0 copy-start.5
  1.3 0.6 %copy-done.6 = f32[128]{0:T(128)S(1)} copy-done((f32[128]{0:T(128)S(1)}, f32[128]{0:T(128)}, u32[]{:S(2)}) %copy-start.6) | copy-done | bytes 536
  1.9 0.0 copy-done.7
  2.0 0.0 copy-done.2
  2.0 0.0 copy-done.3
  2.0 0.0 copy-done.4
  2.0 0.0 copy-done.5
  2.0 0.0 copy-start
  2.0 0.9 %copy-done = bf16[1,1024,128]{2,1,0:T(8,128)(2,1)S(1)} copy-done((bf16[1,1024,128]{2,1,0:T(8,128)(2,1)S(1)}, bf16[1,1024,128]{2,1,0:T(8,128)(2,1)}, u32[]{:S(2)}) %copy-start) | copy-done | bytes 262168
  3.0 0.0 copy-start.1
  3.0 0.7 %copy-done.1 = f32[3,1024]{1,0:T(4,128)S(1)} copy-done((f32[3,1024]{1,0:T(4,128)S(1)}, f32[3,1024]{1,0:T(4,128)}, u32[]{:S(2)}) %copy-start.1) | copy-done | bytes 12312
  3.7 18.7 %shard_map.104 = (bf16[1,128,128]{2,1,0:T(8,128)(2,1)S(1)}, f32[1,16,128]{2,1,0:T(8,128)S(1)}) custom-call(f32[1]{0:T(128)S(6)} %copy.13.wave, f32[3,1024]{1,0:T(4,128)S(1)} %copy-done.1, bf16[1,1024,128]{2,1,0:T(8,128)(2,1)S(1)} %copy-done, f32[3,128]{1,0:T(4,128)S(1)} %copy-done.2, f32[1,128]{1,0:T(1,128)S(1)} %bitcast.5, s32[1,128]{1,0:T(1,128)S(1)} %bitcast.6, ...), custom_call_target="tpu_custom_call" | custom-call | tf_op jit(solution)/shard_map/pallas_call | solution.py:271
  22.4 0.6 %copy.14 = bf16[1,128,128]{2,1,0:T(8,128)(2,1)} copy(bf16[1,128,128]{2,1,0:T(8,128)(2,1)S(1)} %get-tuple-element.4) | data formatting | bytes 65536
  23.0 0.6 %copy.15 = f32[1,16,128]{2,1,0:T(8,128)} copy(f32[1,16,128]{2,1,0:T(8,128)S(1)} %get-tuple-element.5) | data formatting | bytes 16384
Async XLA Ops:
  1.3 0.7 %copy-start.6 = (f32[128]{0:T(128)S(1)}, f32[128]{0:T(128)}, u32[]{:S(2)}) copy-start(f32[128]{0:T(128)} %param.15) | copy-start | bytes 1540
  1.3 0.7 %copy-start.7 = (f32[128]{0:T(128)S(1)}, f32[128]{0:T(128)}, u32[]{:S(2)}) copy-start(f32[128]{0:T(128)} %param.16) | copy-start | bytes 1540
  1.3 0.7 %copy-start.2 = (f32[3,128]{1,0:T(4,128)S(1)}, f32[3,128]{1,0:T(4,128)}, u32[]{:S(2)}) copy-start(f32[3,128]{1,0:T(4,128)} %main_pts.1) | copy-start | bytes 4612
  1.3 0.7 %copy-start.3 = (f32[128]{0:T(128)S(1)}, f32[128]{0:T(128)}, u32[]{:S(2)}) copy-start(f32[128]{0:T(128)} %param.12) | copy-start | bytes 1540
  1.3 0.7 %copy-start.4 = (s32[128]{0:T(128)S(1)}, s32[128]{0:T(128)}, u32[]{:S(2)}) copy-start(s32[128]{0:T(128)} %param.13) | copy-start | bytes 1540
  1.3 0.7 %copy-start.5 = (f32[64]{0:T(128)S(1)}, f32[64]{0:T(128)}, u32[]{:S(2)}) copy-start(f32[64]{0:T(128)} %param.14) | copy-start | bytes 772
  2.0 0.9 %copy-start = (bf16[1,1024,128]{2,1,0:T(8,128)(2,1)S(1)}, bf16[1,1024,128]{2,1,0:T(8,128)(2,1)}, u32[]{:S(2)}) copy-start(bf16[1,1024,128]{2,1,0:T(8,128)(2,1)} %sub_cur.1) | copy-start | bytes 786436
  3.0 0.7 %copy-start.1 = (f32[3,1024]{1,0:T(4,128)S(1)}, f32[3,1024]{1,0:T(4,128)}, u32[]{:S(2)}) copy-start(f32[3,1024]{1,0:T(4,128)} %sub_pts.1) | copy-start | bytes 36868

commit v2 on v1

v2 whole, which is shorter than its diff:
```python
import functools
import math

import jax
import jax.numpy as jnp
from jax import lax
from jax.experimental import pallas as pl
from jax.experimental.pallas import tpu as pltpu
from jax.sharding import PartitionSpec as P

MESH = pl.DeviceIdType.MESH
VMEM_MIB = 56
TURN = 2.0 * math.pi
COS_HALF = (1.4142135381698608, -6.978850841522217, 5.739460468292236, -1.8835580348968506, 0.3106880187988281)
SIN_HALF = (4.442879676818848, -7.307816505432129, 3.5977745056152344, -0.7911993861198425)


def poly(coefs, s):
    value = coefs[-1]
    for coef in coefs[-2::-1]:
        value = value * s + coef
    return value


def turn_cos_sin(t):
    f = t - jnp.round(t)
    s = f * f
    half_cos = poly(COS_HALF, s)
    half_sin = f * poly(SIN_HALF, s)
    return 1.0 - half_sin * half_sin, half_cos * half_sin


def each(count, body, start=0):
    if count <= 16:
        for i in range(start, count):
            body(i)
    else:
        lax.fori_loop(start, count, lambda i, c: (body(i), c)[1], 0)


def thirds(x):
    first = x.astype(jnp.bfloat16).astype(jnp.float32)
    rest = x - first
    second = rest.astype(jnp.bfloat16).astype(jnp.float32)
    return first, second, rest - second


def left_rows(x):
    a, b, c = thirds(x)
    return jnp.concatenate([a, a, b, b, a, c], 0)


def right_rows(x):
    a, b, c = thirds(x)
    return jnp.concatenate([a, b, a, b, c, a], 0).astype(jnp.bfloat16)


def stack_rows(rows):
    n = rows[0].shape[1]
    index = lax.broadcasted_iota(jnp.int32, (8, n), 0)
    out = jnp.zeros((8, n), jnp.float32)
    for i, row in enumerate(rows):
        out = jnp.where(index == i, row, out)
    return out


def columns(rows):
    return jnp.transpose(stack_rows(rows))


def left_side(x):
    return jnp.transpose(left_rows(x)).astype(jnp.bfloat16)


def swapped(x):
    return pltpu.roll(x, x.shape[1] // 2, 1)


def paired(value, step, count):
    bit = 1
    while bit < count:
        value = value + bit * (step // bit % 2) * (1 - 2 * (value // bit % 2))
        bit *= 2
    return value


def kernel(
    S, T, sub_total, main_total,
    wave, sub_pts, sub_cur, main_pts, weight, ids, shift, theta, phi,
    cur_out, far_out,
    v_sub, v_cur, v_main, v_weight, v_ids, v_shift, v_theta, v_phi,
    pack, r2, kern, fkern, current, own, part, part_in, rad_sum, rad_own, rad_out, rad_in, turn_cols, cur_cols,
    in_sem, x_send, x_recv, a_send, a_recv, b_send, b_recv, c_send, c_recv,
):
    rows = main_pts.shape[1]
    half = rows // 2
    dirs = theta.shape[1]
    cols = sub_cur.shape[2]
    src, tgt, pol = lax.axis_index("src"), lax.axis_index("tgt"), lax.axis_index("pol")
    N = S * T * 2
    own_rows = dirs // (S * T)
    flat = (src * T + tgt) * 2 + pol
    bf16, f32 = jnp.bfloat16, jnp.float32

    def member(d):
        other = paired(flat, d, N)
        return other, {"src": other // (T * 2), "tgt": other // 2 % T, "pol": other % 2}

    loads = [
        pltpu.make_async_copy(a, b, in_sem.at[i])
        for i, (a, b) in enumerate([
            (main_pts, v_main), (weight, v_weight), (ids, v_ids), (shift, v_shift),
            (sub_cur.at[0], v_cur.at[pol]), (sub_pts, v_sub), (theta, v_theta), (phi, v_phi),
        ])
    ]
    for load in loads:
        load.start()
    barrier = pltpu.get_barrier_semaphore()

    def greet(d):
        pl.semaphore_signal(barrier, inc=1, device_id=member(d)[1], device_id_type=MESH)

    each(S, lambda i: greet(i * (2 * T)), 1)
    each(S, lambda i: each(2 * T, lambda j: greet(i * (2 * T) + j), 1))

    for load in loads[:4]:
        load.wait()
    q = wave[0] * (1.0 / TURN)
    sign = jnp.where(lax.broadcasted_iota(jnp.int32, (1, cols), 1) < cols // 2, 1.0, -1.0)
    lower = pol == 0

    def own_half(row):
        return jnp.where(lower, row[:, :half], row[:, half:])

    panels = shift.shape[1]
    panel = lax.broadcasted_iota(jnp.int32, (panels, rows), 0)
    shift_col = jnp.transpose(stack_rows([v_shift[...]]))[:, 0:1]
    chosen = jnp.sum(jnp.where(v_ids[...] == panel, shift_col, 0.0), 0, keepdims=True)
    cos_a, sin_a = turn_cos_sin(2.0 * q * chosen)
    factor = (1.0 / math.sqrt(sub_total)) * v_weight[...]
    fact_cos, fact_sin = factor * cos_a, factor * sin_a
    x, y, z = (v_main[i : i + 1, :] * q for i in range(3))
    pack[0] = stack_rows([
        own_half(row)
        for row in (-2.0 * x, -2.0 * y, -2.0 * z, x * x + y * y + z * z, jnp.ones_like(x), fact_cos, fact_sin)
    ])
    loads[4].wait()
    pl.semaphore_wait(barrier, N - 1)

    def points_copy(d):
        return pltpu.make_async_remote_copy(
            pack.at[0], pack.at[d], a_send.at[d], a_recv.at[d],
            device_id={"src": paired(src, d, S)}, device_id_type=MESH,
        )

    each(S, lambda d: points_copy(d).start(), 1)
    exchange = pltpu.make_async_remote_copy(
        v_cur.at[pol], v_cur.at[pol], x_send.at[0], x_recv.at[0],
        device_id={"pol": 1 - pol}, device_id_type=MESH,
    )
    exchange.start()
    for load in loads[5:]:
        load.wait()

    sx, sy, sz = (v_sub[i : i + 1, :] * q for i in range(3))
    sub_side = right_rows(
        stack_rows([sx, sy, sz, jnp.ones_like(sx), sx * sx + sy * sy + sz * sz])
    )
    cos_t, sin_t = turn_cos_sin(v_theta[...] * (1.0 / TURN))
    cos_p, sin_p = turn_cos_sin(v_phi[...] * (1.0 / TURN))
    phi_cols = columns([cos_p, sin_p])
    far_scale = 1.0 / math.sqrt(main_total)
    turn_cols[0] = jnp.broadcast_to(phi_cols[:, 0:1] * far_scale, (dirs, cols))
    turn_cols[1] = jnp.broadcast_to(phi_cols[:, 1:2] * far_scale, (dirs, cols))
    unit_side = left_side(stack_rows([-0.5 * sin_t * cos_p, -0.5 * sin_t * sin_p, -0.5 * cos_t]))
    fact_cols = columns([fact_cos, fact_sin])
    cur_cols[0] = jnp.broadcast_to(fact_cols[:, 0:1], (rows, cols))
    cur_cols[1] = fact_cols[:, 1:2] * sign
    step = 128

    def far_kernels(j):
        turns = jnp.dot(
            unit_side,
            right_rows(jnp.concatenate([pack[2 * j], pack[2 * j + 1]], 1)),
            preferred_element_type=f32,
        )
        for at in range(0, dirs, step):
            cosine, sine = turn_cos_sin(turns[at : at + step])
            fkern[j, at : at + step, :] = cosine.astype(bf16)
            fkern[j, dirs + at : dirs + at + step, :] = sine.astype(bf16)

    def part_copy(d, k):
        to = pol if k == 0 else 1 - pol
        return pltpu.make_async_remote_copy(
            part.at[d, to], part_in.at[2 * d + k], b_send.at[2 * d + k], b_recv.at[2 * d + k],
            device_id={"src": paired(src, d, S), "pol": to}, device_id_type=MESH,
        )

    def near_block(slots):
        packed = [pack[d] for d in slots]
        packed = packed[0] if len(packed) == 1 else jnp.concatenate(packed, 1)
        count = half * len(slots)
        turned = jnp.transpose(jnp.concatenate([left_rows(packed), packed], 0))
        r2[:count] = jnp.dot(turned[:, :48].astype(bf16), sub_side, preferred_element_type=f32)
        size = 16
        for at in range(0, count, size):
            square = r2[at : at + size, :]
            inverse = lax.rsqrt(square)
            cosine, sine = turn_cos_sin(square * inverse)
            inverse = inverse * (4.0 * q)
            kern[at : at + size, :] = (cosine * inverse).astype(bf16)
            kern[count + at : count + at + size, :] = (sine * inverse).astype(bf16)
        if len(slots) == 1 and slots[0] == 0:
            exchange.wait_recv()
        both = jnp.dot(
            kern[: 2 * count], jnp.concatenate([v_cur[0], v_cur[1]], 1), preferred_element_type=f32
        )
        fields, currents = [], []
        for c in (0, cols):
            field = both[:count, c : c + cols] + sign * swapped(both[count:, c : c + cols])
            fields.append(field)
            currents.append(
                (field * turned[:, 53:54] + swapped(field) * (turned[:, 54:55] * sign)).astype(bf16)
            )
        for i, d in enumerate(slots):
            at = slice(i * half, (i + 1) * half)
            for c in (0, 1):
                part[d, c] = fields[c][at].astype(bf16)
                current[d, :, c * cols : (c + 1) * cols] = currents[c][at]
            if isinstance(d, int) and d == 0:
                own[0], own[1] = fields[0], fields[1]
            else:
                part_copy(d, 0).start()
            part_copy(d, 1).start()

    def far_product(j):
        return jnp.dot(
            fkern[j],
            jnp.concatenate([current[2 * j], current[2 * j + 1]], 0),
            preferred_element_type=f32,
        )

    near_block((0,))
    if S <= 16:
        for j in range(1, S // 2):
            points_copy(2 * j).wait_recv()
            points_copy(2 * j + 1).wait_recv()
            near_block((2 * j, 2 * j + 1))
            far_kernels(j)
    else:

        def pair_step(j, c):
            points_copy(2 * j).wait_recv()
            points_copy(2 * j + 1).wait_recv()
            near_block((2 * j, 2 * j + 1))
            far_kernels(j)
            return c

        lax.fori_loop(1, S // 2, pair_step, 0)
    points_copy(1).wait_recv()
    near_block((1,))
    far_kernels(0)
    rad_sum[...] = far_product(0)

    def add_pair(j):
        rad_sum[...] += far_product(j)

    each(S // 2, add_pair, 1)
    for at in range(0, dirs, step):
        real = rad_sum[at : at + step]
        imag = rad_sum[dirs + at : dirs + at + step]
        first, second = (
            real[:, c : c + cols] - sign * swapped(imag[:, c : c + cols]) for c in (0, cols)
        )
        cosine, sine = turn_cols[0, at : at + step], turn_cols[1, at : at + step]
        co_polar = cosine * first + sine * second
        cross_polar = cosine * second - sine * first
        rad_own[0, at : at + step] = co_polar
        rad_own[1, at : at + step] = cross_polar
        rad_out[0, at : at + step] = co_polar.astype(bf16)
        rad_out[1, at : at + step] = cross_polar.astype(bf16)

    def far_copy(d):
        other, where = member(d)
        first = pl.multiple_of(other // 2 * own_rows, own_rows)
        return pltpu.make_async_remote_copy(
            rad_out.at[other % 2, pl.ds(first, own_rows)], rad_in.at[d], c_send.at[d], c_recv.at[d],
            device_id=where, device_id_type=MESH,
        )

    each(N, lambda i: far_copy(N - i).start(), 1)

    exchange.wait_send()
    each(S, lambda d: points_copy(d).wait_send(), 1)
    part_copy(0, 1).wait_send()
    each(S, lambda d: (part_copy(d, 0).wait_send(), part_copy(d, 1).wait_send()), 1)
    for k in (0, 1):
        if k == 0:
            induced = own[pol]
        else:
            part_copy(0, 1).wait_recv()
            induced = part_in[1].astype(f32)

        def added(d, total):
            part_copy(d, k).wait_recv()
            return total + part_in[2 * d + k].astype(f32)

        if S <= 16:
            for d in range(1, S):
                induced = added(d, induced)
        else:
            induced = lax.fori_loop(1, S, added, induced)
        there = pl.ds(pl.multiple_of((pol if k == 0 else 1 - pol) * half, half), half)
        cur_out[0, there] = (
            induced * cur_cols[0, there] + swapped(induced) * cur_cols[1, there]
        ).astype(bf16)

    each(N, lambda d: far_copy(d).wait(), 1)
    here = pl.ds(pl.multiple_of((src * T + tgt) * own_rows, own_rows), own_rows)
    total = rad_own[pol, here]
    if N <= 16:
        for d in range(1, N):
            total = total + rad_in[d].astype(f32)
    else:
        total = lax.fori_loop(1, N, lambda d, t: t + rad_in[d].astype(f32), total)
    far_out[0] = total


def on_device(S, T, sub_points, sub_currents, main_points, main_weight, panel_ids, panel_shift, theta, phi, wavenumber):
    rows, subs = main_points.shape[1], sub_points.shape[1]
    half = rows // 2
    cols = sub_currents.shape[2]
    dirs = theta.shape[0]
    panels = panel_shift.shape[0]
    N = S * T * 2
    own_rows = dirs // (S * T)
    f32, bf16 = jnp.float32, jnp.bfloat16
    hbm = pl.BlockSpec(memory_space=pl.ANY)
    vmem = pl.BlockSpec(memory_space=pltpu.VMEM)
    dma = pltpu.SemaphoreType.DMA
    return pl.pallas_call(
        functools.partial(kernel, S, T, subs * S, rows * S * T),
        out_shape=(
            jax.ShapeDtypeStruct((1, rows, cols), bf16),
            jax.ShapeDtypeStruct((1, own_rows, cols), f32),
        ),
        in_specs=[pl.BlockSpec(memory_space=pltpu.SMEM)] + [hbm] * 8,
        out_specs=(vmem, vmem),
        scratch_shapes=[
            pltpu.VMEM((3, subs), f32),
            pltpu.VMEM((2, subs, cols), bf16),
            pltpu.VMEM((3, rows), f32),
            pltpu.VMEM((1, rows), f32),
            pltpu.VMEM((1, rows), jnp.int32),
            pltpu.VMEM((1, panels), f32),
            pltpu.VMEM((1, dirs), f32),
            pltpu.VMEM((1, dirs), f32),
            pltpu.VMEM((S, 8, half), f32),
            pltpu.VMEM((rows, subs), f32),
            pltpu.VMEM((2 * rows, subs), bf16),
            pltpu.VMEM((S // 2, 2 * dirs, rows), bf16),
            pltpu.VMEM((S, half, 2 * cols), bf16),
            pltpu.VMEM((2, half, cols), f32),
            pltpu.VMEM((S, 2, half, cols), bf16),
            pltpu.VMEM((2 * S, half, cols), bf16),
            pltpu.VMEM((2 * dirs, 2 * cols), f32),
            pltpu.VMEM((2, dirs, cols), f32),
            pltpu.VMEM((2, dirs, cols), bf16),
            pltpu.VMEM((N, own_rows, cols), bf16),
            pltpu.VMEM((2, dirs, cols), f32),
            pltpu.VMEM((2, rows, cols), f32),
            dma((8,)),
            dma((1,)),
            dma((1,)),
            dma((S,)),
            dma((S,)),
            dma((2 * S,)),
            dma((2 * S,)),
            dma((N,)),
            dma((N,)),
        ],
        compiler_params=pltpu.CompilerParams(
            collective_id=0, has_side_effects=True, vmem_limit_bytes=VMEM_MIB * 1024 * 1024
        ),
    )(
        wavenumber, sub_points, sub_currents, main_points, main_weight.reshape(1, -1),
        panel_ids.reshape(1, -1), panel_shift.reshape(1, -1), theta.reshape(1, -1), phi.reshape(1, -1),
    )


def solution(mesh):
    placed = (
        P(None, "src"),
        P("pol", "src", None),
        P(None, ("src", "tgt")),
        P(("src", "tgt")),
        P(("src", "tgt")),
        P(),
        P(),
        P(),
        P("freq"),
    )
    return jax.shard_map(
        functools.partial(on_device, mesh.shape["src"], mesh.shape["tgt"]),
        mesh=mesh,
        in_specs=placed,
        out_specs=(P("pol", ("src", "tgt"), "freq"), P("pol", ("src", "tgt"), "freq")),
        check_vma=False,
    )
```

time: 23.8 us -> 21.4 us (0.90)
  local copies, waits for them, and re-layouts: 3.57 us -> 1.98 us
  Pallas kernels: 18.7 us -> 17.9 us
    unnamed x18 -> x4, local copies, waits for them, and re-layouts: 3.57 us -> 1.98 us
    pallas_call x1, Pallas kernels: 18.7 us -> 17.9 us  [on_device(): pl.pallas_call(functools.partial(kernel, S, T, subs * S, rows * S * T), o...]
where the time goes in v2:
time: 21.4 us; the launch traced here: 21.2 us
  Pallas kernels  17.9 us (84%)
  local copies, waits for them, and re-layouts  1.98 us (9%)
  between operations  1.3 us (6%)
    pallas_call x1, Pallas kernels, on_device(): pl.pallas_call(functools.partial(kernel, S, T, subs * S, rows * S * T), o...  17.9 us
    unnamed x4, local copies, waits for them, and re-layouts  1.98 us

profile of v2, /device:TPU:0, one launch (start us, length us, event | category | flops | bytes accessed | tf_op | source)
XLA Modules:
  0.0 21.2 jit_solution(2629424741023316419)
XLA Ops:
  1.3 17.9 %shard_map.104 = (bf16[1,128,128]{2,1,0:T(8,128)(2,1)}, f32[1,16,128]{2,1,0:T(8,128)}) custom-call(f32[1]{0:T(128)S(6)} %copy.13.wave, f32[3,1024]{1,0:T(4,128)} %sub_pts.1, bf16[1,1024,128]{2,1,0:T(8,128)(2,1)} %sub_cur.1, f32[3,128]{1,0:T(4,128)} %main_pts.1, f32[1,128]{1,0:T(1,128)} %bitcast.5, s32[1,128]{1,0:T(1,128)} %bitcast.6, f32[1,64]{1,0:T(1,128)} %bitcast.7, ...), custom_call_target="tpu_custom_call" | custom-call | tf_op jit(solution)/shard_map/pallas_call | solution.py:341
  19.2 0.0 copy-start
  19.2 1.4 %copy.14 = bf16[1,128,128]{2,1,0:T(8,128)(2,1)} copy(bf16[1,128,128]{2,1,0:T(8,128)(2,1)} %get-tuple-element.4) | data formatting | bytes 65536
  20.6 0.0 copy-done
  20.6 0.6 %copy.15 = f32[1,16,128]{2,1,0:T(8,128)} copy(f32[1,16,128]{2,1,0:T(8,128)S(1)} %copy-done) | data formatting | bytes 16384
Async XLA Ops:
  19.2 1.4 %copy-start = (f32[1,16,128]{2,1,0:T(8,128)S(1)}, f32[1,16,128]{2,1,0:T(8,128)}, u32[]{:S(2)}) copy-start(f32[1,16,128]{2,1,0:T(8,128)} %get-tuple-element.5) | copy-start | bytes 24580
